TPU v7x, 128 devices: a whole 4x4x4 slice. The times are simulated.
128 devices in a mesh: rep: 8 (over x, core), head: 4 (over y), side: 4 (over z).
Axes of the slice: x: 4, y: 4, z: 4, core: 2. Of those that a mesh axis runs over, the one named last changes fastest.
Arguments:
- tokens: bfloat16 [8192, 7168], P(('rep', 'head', 'side')), may hold values from -6 to 6
- routes: int32 [8192, 2], P(('rep', 'head', 'side')), may hold values from 0 to 31, all different within a row; in each aligned block of 64 rows (0 to 63, 64 to 127, ...) at most 8 rows name the same one
- gates: float32 [8192, 2], P(('rep', 'head', 'side')), may hold values from 0.2 to 1.5
- w_gate: bfloat16 [32, 7168, 2048], P(('rep', 'head'), None, 'side'), may hold values from -0.0625 to 0.0625
- w_up: bfloat16 [32, 7168, 2048], P(('rep', 'head'), None, 'side'), may hold values from -0.0625 to 0.0625
- w_down: bfloat16 [32, 2048, 7168], P(('rep', 'head'), 'side'), may hold values from -0.125 to 0.125
Outputs:
- moe_out: bfloat16 [8192, 7168], P(('rep', 'head', 'side'))
Inputs may be any that keep to these rules, and one draw needn't show every extreme that they name: `routes`: within the rows of one device no expert is named more than 8 times, and in every draw some device names some expert exactly 8 times; a token's 2 experts differ.
All inputs are finite; a program needn't handle non-finite values.
Results may differ from a plain program's by a relative error of at most 0.017.
Values may be sent and summed in bfloat16 or wider, within the bound.
A program may use at most 128 MiB of HBM per device.

v0:
```python
import jax
import jax.numpy as jnp
from jax import lax
from jax.sharding import PartitionSpec as P


def on_device(tokens, routes, gates, w_gate, w_up, w_down):
    tok_rows = tokens.shape[0]
    width = tokens.shape[1]
    fanout = routes.shape[1]
    owners = lax.axis_size(("rep", "head"))
    per_owner = w_gate.shape[0]
    experts = owners * per_owner
    capacity = max(2, 2 * tok_rows * fanout // experts)
    flat_routes = routes.reshape(-1)
    onehot = (flat_routes[:, None] == jnp.arange(experts)[None, :]).astype(jnp.int32)
    before = jnp.cumsum(onehot, axis=0) - onehot
    slot_index = jnp.sum(before * onehot, axis=1)
    target = flat_routes * capacity + slot_index
    picker = (target[:, None] == jnp.arange(experts * capacity)[None, :]).astype(jnp.bfloat16)
    token_picker = jnp.sum(picker.reshape(tok_rows, fanout, experts * capacity), axis=1)
    outgoing = jnp.einsum("ts,td->sd", token_picker, tokens, preferred_element_type=jnp.float32)
    outgoing = outgoing.astype(jnp.bfloat16).reshape(owners, per_owner, capacity, width)
    arrived = lax.all_to_all(outgoing, ("rep", "head"), split_axis=0, concat_axis=0, tiled=True)
    rows_all = lax.all_gather(arrived, "side", axis=0, tiled=True)
    gate_proj = jnp.einsum("gecd,edh->gech", rows_all, w_gate, preferred_element_type=jnp.float32)
    up_proj = jnp.einsum("gecd,edh->gech", rows_all, w_up, preferred_element_type=jnp.float32)
    hidden = (jax.nn.silu(gate_proj) * up_proj).astype(jnp.bfloat16)
    summed = lax.psum_scatter(
        jnp.einsum("gech,ehd->gecd", hidden, w_down, preferred_element_type=jnp.float32).astype(
            jnp.bfloat16
        ),
        "side",
        scatter_dimension=0,
        tiled=True,
    )
    returned_rows = lax.all_to_all(summed, ("rep", "head"), split_axis=0, concat_axis=0, tiled=True)
    returned_flat = returned_rows.reshape(experts * capacity, width)
    picked = jnp.dot(picker, returned_flat, preferred_element_type=jnp.float32)
    picked = picked.reshape(tok_rows, fanout, width)
    return jnp.sum(picked * gates[:, :, None], axis=1).astype(jnp.bfloat16)


def solution(mesh):
    placed = (
        P(("rep", "head", "side"), None),
        P(("rep", "head", "side"), None),
        P(("rep", "head", "side"), None),
        P(("rep", "head"), None, "side"),
        P(("rep", "head"), None, "side"),
        P(("rep", "head"), "side", None),
    )
    return jax.shard_map(
        on_device,
        mesh=mesh,
        in_specs=placed,
        out_specs=P(("rep", "head", "side"), None),
        check_vma=False,
    )
```

profile of v0, /device:TPU:1, one launch (start us, length us, event | category | flops | bytes accessed | tf_op | source)
XLA Modules:
  0.0 436.0 jit_solution(10895905577242654201)
XLA Ops:
  6.5 0.0 copy-start
  6.5 0.0 all-gather.2.cloned.1.call-start
  6.5 0.8 copy.33
  7.4 0.1 eq.51
  7.5 0.1 fusion.30
  7.6 0.2 reduce_window_sum.11
  7.8 0.2 select_reduce_fusion
  8.0 0.1 reduce_sum.33
  8.1 0.1 copy.34
  8.2 0.7 multiply_add_fusion
  8.9 0.1 fusion.28
  9.0 0.0 copy-done
  9.0 1.1 fusion.4
  10.1 53.4 %all_to_all.10 = bf16[32,1,8,7168]{3,2,1,0:T(8,128)(2,1)S(1)} all-to-all(bf16[32,1,8,7168]{3,2,1,0:T(8,128)(2,1)S(1)} %fusion.4), channel_id=1, replica_groups=mesh['rep'=8,'head'=4,'side'=4] {'rep','head'}, dimensions={0} | all-to-all | bytes 7340032 | tf_op jit(solution)/shard_map/all_to_all | solution.py:24
  63.5 3.8 copy.36
  67.3 0.0 all-gather.2.cloned.1.call-update
  67.3 0.2 reduce-scatter.2.cloned.1.call-start
  67.5 135.4 %all-gather.2.cloned.1.call-done = bf16[128,1,8,7168]{3,0,2,1:T(8,128)(2,1)} async-done(((bf16[32,1,8,7168]{3,0,2,1:T(8,128)(2,1)}), bf16[128,1,8,7168]{3,0,2,1:T(8,128)(2,1)}) %all-gather.2.cloned.1.call-update) | async-done | bytes 14680080 | tf_op jit(solution)/shard_map/all_gather | solution.py:25
  203.0 0.0 copy-start.3
  203.0 0.0 slice-start
  203.0 13.2 %fusion = f32[128,8,512]{2,0,1:T(8,128)S(1)} fusion(bf16[128,1,8,7168]{3,0,2,1:T(8,128)(2,1)} %all-gather.2.cloned.1.call-done, bf16[1,7168,512]{2,1,0:T(8,128)(2,1)} %param.10), kind=kOutput, calls=%fused_computation | convolution fusion | flops 7516192768 | bytes 24117248 | tf_op jit(solution)/shard_map/gecd,edh->gech/dot_general | solution.py:27
  216.2 0.0 copy-done.3
  216.2 0.0 slice-start.1
  216.3 10.3 %fusion.20 = bf16[128,8,512]{2,0,1:T(8,128)(2,1)S(1)} fusion(f32[128,8,512]{2,0,1:T(8,128)S(1)} %fusion, bf16[1,7168,512]{2,1,0:T(8,128)(2,1)} %param.9, bf16[128,1,8,7168]{3,0,2,1:T(8,128)(2,1)S(1)} %copy-done.3), kind=kOutput, calls=%fused_computation.20 | convolution fusion | flops 7519338496 | bytes 25165824 | tf_op jit(solution)/shard_map/gecd,edh->gech/dot_general | solution.py:26
  226.5 0.0 slice-done
  226.5 0.0 slice-done.1
  226.6 11.1 %convert_bitcast_fusion = bf16[128,1,8,7168]{3,0,2,1:T(8,128)(2,1)} fusion(bf16[128,8,512]{2,0,1:T(8,128)(2,1)S(1)} %fusion.20, bf16[1,512,7168]{2,1,0:T(8,128)(2,1)S(1)} %bitcast.80), kind=kOutput, calls=%fused_computation.4 | convolution fusion | flops 7523532800 | bytes 23068672 | tf_op jit(solution)/shard_map/gech,ehd->gecd/dot_general | solution.py:30
  237.6 0.0 reduce-scatter.2.cloned.1.call-update
  237.7 132.9 %reduce-scatter.2.cloned.1.call-done = bf16[32,1,8,7168]{3,0,2,1:T(8,128)(2,1)} async-done(((bf16[128,1,8,7168]{3,0,2,1:T(8,128)(2,1)}), bf16[32,1,8,7168]{3,0,2,1:T(8,128)(2,1)}) %reduce-scatter.2.cloned.1.call-update) | async-done | bytes 3670032 | tf_op jit(solution)/shard_map/reduce_scatter | solution.py:29
  370.6 4.0 copy.37
  374.6 0.0 copy-start.2
  374.6 0.0 copy-start.1
  374.7 52.4 %all_to_all.11 = bf16[32,1,8,7168]{3,2,1,0:T(8,128)(2,1)S(1)} all-to-all(bf16[32,1,8,7168]{3,2,1,0:T(8,128)(2,1)S(1)} %copy.37), channel_id=1, replica_groups=mesh['rep'=8,'head'=4,'side'=4] {'rep','head'}, dimensions={0} | all-to-all | bytes 7340032 | tf_op jit(solution)/shard_map/all_to_all | solution.py:37
  427.0 0.0 copy-done.2
  427.0 2.1 fusion.13
  429.1 0.0 copy-done.1
  (1 shorter events, 0.0 us)
Async XLA Ops:
  6.5 2.5 copy-start
  6.5 196.4 %all-gather.2.cloned.1.call-start = ((), (), s32[]{:S(2)}) async-start(), calls=%async_computation.3 | async-start | bytes 18350080 | tf_op jit(solution)/shard_map/all_gather | solution.py:25
  67.3 303.3 %reduce-scatter.2.cloned.1.call-start = ((), (), s32[]{:S(2)}) async-start(), calls=%async_computation.4 | async-start | bytes 18350080 | tf_op jit(solution)/shard_map/reduce_scatter | solution.py:29
  203.0 13.3 %copy-start.3 = (bf16[128,1,8,7168]{3,0,2,1:T(8,128)(2,1)S(1)}, bf16[128,1,8,7168]{3,0,2,1:T(8,128)(2,1)}, u32[]{:S(2)}) copy-start(bf16[128,1,8,7168]{3,0,2,1:T(8,128)(2,1)} %all-gather.2.cloned.1.call-done) | copy-start | bytes 44040196
  203.0 23.6 %slice-start = ((s8[7340032]{0:T(1024)(128)(4,1)}), s8[4194304]{0:T(1024)(128)(4,1)S(1)}, s32[]{:S(2)}) async-start(s8[7340032]{0:T(1024)(128)(4,1)} %bitcast.79), calls=%async_computation.5 | async-start | bytes 8388608
  216.2 10.3 %slice-start.1 = ((s8[7340032]{0:T(1024)(128)(4,1)}), s8[3145728]{0:T(1024)(128)(4,1)S(1)}, s32[]{:S(2)}) async-start(s8[7340032]{0:T(1024)(128)(4,1)} %bitcast.79), calls=%async_computation.6 | async-start | bytes 6291456
  374.6 52.4 %copy-start.2 = (f32[64,2]{0,1:T(2,128)S(1)}, f32[64,2]{0,1:T(2,128)}, u32[]{:S(2)}) copy-start(f32[64,2]{0,1:T(2,128)} %param.8) | copy-start | bytes 1540
  374.6 54.5 %copy-start.1 = (bf16[64,7168]{1,0:T(8,128)(2,1)S(1)}, bf16[64,7168]{1,0:T(8,128)(2,1)}, u32[]{:S(2)}) copy-start(bf16[64,7168]{1,0:T(8,128)(2,1)} %param.6) | copy-start | bytes 2752516
Sparse Core Ops, SparseCore 0:
  67.4 135.5 all-gather.1
  237.8 132.7 reduce-scatter.1
where the time goes:
time: 436 us
  waiting for transfers between devices  268 us (61%)
  blocking collectives  106 us (24%)
  matrix products  37.8 us (9%)
  between operations  13.5 us (3%)
  local copies, waits for them, and re-layouts  9.07 us (2%)
    all_gather x1, waiting for transfers between devices, on_device(): rows_all = lax.all_gather(arrived, 'side', axis=0, tiled=True)  135 us
    reduce_scatter x1, waiting for transfers between devices, on_device(): lax.psum_scatter(jnp.einsum('gech,ehd->gecd', hidden, w_down, preferred_e...  133 us
    all_to_all x1, blocking collectives, on_device(): lax.all_to_all(outgoing, ('rep', 'head'), split_axis=0, concat_axis=0, ti...  53.4 us
    all_to_all x1, blocking collectives, on_device(): lax.all_to_all(summed, ('rep', 'head'), split_axis=0, concat_axis=0, tile...  52.4 us
    dot_general x1, matrix products, on_device(): jnp.einsum('gecd,edh->gech', rows_all, w_up, preferred_element_type=jnp.f...  13.2 us
    dot_general x1, matrix products, on_device(): jnp.einsum('gech,ehd->gecd', hidden, w_down, preferred_element_type=jnp.f...  11.1 us
    dot_general x1, matrix products, on_device(): jnp.einsum('gecd,edh->gech', rows_all, w_gate, preferred_element_type=jnp...  10.3 us
  transfers between devices with their start and end apart: 2, of which 2 were waited for; matrix products, arithmetic and copies ran while one was open for 0% of the time, Pallas kernels for 0%

commit v1 on v0

v1 whole, which is shorter than its diff:
```python
import functools

import jax
import jax.numpy as jnp
from jax import lax
from jax.experimental import pallas as pl
from jax.experimental.pallas import tpu as pltpu
from jax.sharding import PartitionSpec as P

MESH = pl.DeviceIdType.MESH
F32, BF16 = jnp.float32, jnp.bfloat16
CW = 512
K2 = 4
CAP = 8
TOK = 64
NX, NY, NZ = 4, 4, 4
PLANE = NX * NY
OFFS = [(dx, dy) for dx in range(NX) for dy in range(NY) if (dx, dy) != (0, 0)]


class Place:
    def __init__(self):
        rep = lax.axis_index("rep")
        self.x, self.c = rep // 2, rep % 2
        self.y, self.z = lax.axis_index("head"), lax.axis_index("side")
        self.j = self.x * NY + self.y
        self.up, self.down = lax.rem(self.z + 1, NZ), lax.rem(self.z + NZ - 1, NZ)
        self.core = self.dev(self.x, 1 - self.c, self.y, self.z)
        self.z_up = self.dev(self.x, self.c, self.y, self.up)
        self.z_down = self.dev(self.x, self.c, self.y, self.down)

    def dev(self, x, c, y, z):
        return (x * 2 + c, y, z)

    def plane(self, off):
        x, y = lax.rem(self.x + off[0], NX), lax.rem(self.y + off[1], NY)
        return x * NY + y, self.dev(x, self.c, y, self.z)

    def column(self):
        own = []
        for dc in range(2):
            for dz in range(NZ):
                if (dc, dz) != (0, 0):
                    own.append(self.dev(self.x, lax.rem(self.c + dc, 2), self.y, lax.rem(self.z + dz, NZ)))
        return own


def enter(partners):
    barrier = pltpu.get_barrier_semaphore()
    for device in partners:
        pl.semaphore_signal(barrier, inc=1, device_id=device, device_id_type=MESH)
    pl.semaphore_wait(barrier, len(partners))


def send(src, dst, send_sem, recv_sem, device):
    pltpu.make_async_remote_copy(
        src_ref=src, dst_ref=dst, send_sem=send_sem, recv_sem=recv_sem, device_id=device, device_id_type=MESH
    ).start()


def done(ref, sem):
    pltpu.make_async_copy(ref, ref, sem).wait()


def dispatch_kernel(
    k1, tok, meta, wg_hbm, wu_hbm, hid, gpk,
    tokc, ztok, metas, pk, out1, out2, x1, x2, wg, wu, acc,
    w_sem, m_send, m_recv, c_send, c_recv, t_send, t_recv, tc_send, tc_recv,
    a1_send, a1_recv, z_send, z_recv, f_send, f_recv, a2_send, a2_recv,
):
    me = Place()
    d1 = k1 * CW
    half = TOK // 2
    for kk in range(k1 + K2):
        rows = pl.ds(kk * CW, CW)
        pltpu.make_async_copy(wg_hbm.at[rows], wg.at[rows], w_sem.at[0, kk]).start()
        pltpu.make_async_copy(wu_hbm.at[rows], wu.at[rows], w_sem.at[1, kk]).start()
    enter([me.plane(off)[1] for off in OFFS] + me.column())

    own_meta = metas.at[me.z, me.c]
    pltpu.make_async_copy(meta, own_meta, m_recv).start()
    for i, device in enumerate(me.column()):
        send(meta, own_meta, m_send.at[i], m_recv, device)
    core_rows = pl.ds(pl.multiple_of(me.c * TOK, TOK), TOK)
    for k in range(k1):
        cols = pl.ds(k * CW, CW)
        pltpu.make_async_copy(tok.at[:, cols], tokc.at[k, core_rows], c_recv.at[k]).start()
        send(tok.at[:, cols], tokc.at[k, core_rows], c_send.at[k], c_recv.at[k], me.core)
    tail = pl.ds(d1, K2 * CW)
    own_tok = ztok.at[me.z, core_rows]
    pltpu.make_async_copy(tok.at[:, tail], own_tok, t_recv.at[4]).start()
    send(tok.at[:, tail], own_tok, t_send.at[0], t_recv.at[0], me.z_up)
    send(tok.at[:, tail], own_tok, t_send.at[1], t_recv.at[1], me.z_down)

    done(metas, m_recv)
    shape = (2 * PLANE * CAP, 2 * TOK)
    row = lax.broadcasted_iota(jnp.int32, shape, 0)
    col = lax.broadcasted_iota(jnp.int32, shape, 1)
    dest = row // (2 * CAP)
    want = ((2 * (dest // NY) + me.c) * NY + dest % NY) * CAP + row % CAP
    want = jnp.where((row // CAP) % 2 == col // TOK, want, -1).astype(F32)
    for zz in range(NZ):
        both = metas[zz, 0] + metas[zz, 1]
        hit0, hit1 = want == both[0:1], want == both[1:2]
        pk[zz] = jnp.where(hit0 | hit1, 1.0, 0.0).astype(BF16)
        gated = jnp.where(hit0, both[2:3], 0.0) + jnp.where(hit1, both[3:4], 0.0)
        gated = gated.T
        high = gated.astype(BF16)
        gpk[zz, 0] = high
        gpk[zz, 1] = (gated - high.astype(F32)).astype(BF16)

    def p1_issue(k):
        done(tokc.at[k], c_recv.at[k])
        picked = jnp.dot(pk[me.z], tokc[k], preferred_element_type=F32)
        out1[k] = picked.astype(BF16).reshape(PLANE, 2 * CAP, CW)
        here = x1.at[k, me.z, me.j]
        for off in OFFS:
            j, device = me.plane(off)
            send(out1.at[k, j], here, a1_send.at[k], a1_recv.at[k], device)
        pltpu.make_async_copy(out1.at[k, me.j], here, a1_recv.at[k]).start()

    def z_issue(k):
        block = x1.at[k, me.z]
        done(block, a1_recv.at[k])
        send(block, block, z_send.at[k, 0], z_recv.at[k, 0], me.z_up)
        send(block, block, z_send.at[k, 1], z_recv.at[k, 1], me.z_down)

    def z_forward(k):
        low, high = pl.ds(0, PLANE // 2), pl.ds(PLANE // 2, PLANE // 2)
        done(x1.at[k, me.down], z_recv.at[k, 0])
        part = x1.at[k, me.down, low]
        send(part, part, f_send.at[k, 0], f_recv.at[k, 0], me.z_up)
        done(x1.at[k, me.up], z_recv.at[k, 1])
        part = x1.at[k, me.up, high]
        send(part, part, f_send.at[k, 1], f_recv.at[k, 1], me.z_down)

    def project(block, kk):
        rows = pl.ds(pl.multiple_of(kk * CW, CW), CW)
        done(wg.at[rows], w_sem.at[0, kk])
        done(wu.at[rows], w_sem.at[1, kk])
        hid_cols = wg.shape[1]
        for base, w in ((0, wg), (hid_cols, wu)):
            @pl.loop(0, hid_cols // 256)
            def _(n):
                cols = pl.ds(pl.multiple_of(n * 256, 256), 256)
                to = pl.ds(pl.multiple_of(base + n * 256, 256), 256)
                part = jnp.dot(block[...].reshape(acc.shape[0], CW), w[rows, cols], preferred_element_type=F32)
                acc[:, to] = acc[:, to] + part

    def mm1(k):
        across = lax.rem(me.z + 2, NZ)
        done(x1.at[k, across, pl.ds(0, PLANE // 2)], f_recv.at[k, 0])
        done(x1.at[k, across, pl.ds(PLANE // 2, PLANE // 2)], f_recv.at[k, 1])
        project(x1.at[k], k)

    def p2_issue(m):
        cols = pl.ds(pl.multiple_of(m * CW, CW), CW)

        @pl.loop(0, NZ)
        def _(zz):
            picked = jnp.dot(pk[zz], ztok[zz, :, cols], preferred_element_type=F32)
            out2[m, zz] = picked.astype(BF16).reshape(PLANE, 2 * CAP, CW)

        here = x2.at[m, :, me.j]
        for off in OFFS:
            j, device = me.plane(off)
            send(out2.at[m, :, j], here, a2_send.at[m], a2_recv.at[m], device)
        pltpu.make_async_copy(out2.at[m, :, me.j], here, a2_recv.at[m]).start()

    def mm2(m):
        done(x2.at[m], a2_recv.at[m])
        project(x2.at[m], k1 + m)

    p1_issue(0)
    p1_issue(1)
    done(ztok.at[me.down, core_rows], t_recv.at[0])
    part = ztok.at[me.down, pl.ds(pl.multiple_of(me.c * TOK, TOK), half)]
    send(part, part, t_send.at[2], t_recv.at[2], me.z_up)
    done(ztok.at[me.up, core_rows], t_recv.at[1])
    part = ztok.at[me.up, pl.ds(pl.multiple_of(me.c * TOK + half, half), half)]
    send(part, part, t_send.at[3], t_recv.at[3], me.z_down)
    z_issue(0)
    p1_issue(2)
    acc[...] = jnp.zeros_like(acc)
    across = lax.rem(me.z + 2, NZ)
    done(ztok.at[across, pl.ds(pl.multiple_of(me.c * TOK, TOK), half)], t_recv.at[2])
    done(ztok.at[across, pl.ds(pl.multiple_of(me.c * TOK + half, half), half)], t_recv.at[3])
    done(own_tok, t_recv.at[4])
    mine = ztok.at[:, core_rows]
    send(mine, mine, tc_send, tc_recv, me.core)
    z_issue(1)
    other = ztok.at[:, pl.ds(pl.multiple_of((1 - me.c) * TOK, TOK), TOK)]
    done(other, tc_recv)

    @pl.loop(0, k1 + 2)
    def _(k):
        @pl.when((k % 2 == 0) & (k // 2 < K2))
        def _():
            p2_issue(k // 2)

        @pl.when((k >= 2) & (k < k1))
        def _():
            z_issue(k)

        @pl.when((k >= 1) & (k < k1 + 1))
        def _():
            z_forward(k - 1)

        @pl.when(k + 3 < k1)
        def _():
            p1_issue(k + 3)

        @pl.when(k >= 2)
        def _():
            mm1(k - 2)

        @pl.when((k >= 5) & (k % 2 == 1) & ((k - 5) // 2 < K2))
        def _():
            mm2((k - 5) // 2)

    @pl.loop(0, acc.shape[0] // 128)
    def _(i):
        rows = pl.ds(pl.multiple_of(i * 128, 128), 128)
        hc = wg.shape[1]
        g, u = acc[rows, :hc], acc[rows, hc:]
        hid[rows, :] = (g / (1.0 + jnp.exp(-g)) * u).astype(BF16)

    for i in range(2 * NZ - 1):
        done(meta, m_send.at[i])
    done(tok.at[:, tail], t_send.at[0])
    done(tok.at[:, tail], t_send.at[1])
    done(ztok.at[0, pl.ds(0, half)], t_send.at[2])
    done(ztok.at[0, pl.ds(0, half)], t_send.at[3])
    done(mine, tc_send)

    @pl.loop(0, k1)
    def _(k):
        done(tokc.at[k, pl.ds(0, TOK)], c_send.at[k])
        done(out1.at[k, pl.ds(0, PLANE - 1)], a1_send.at[k])
        for side in range(2):
            done(x1.at[k, 0], z_send.at[k, side])
            done(x1.at[k, 0, pl.ds(0, PLANE // 2)], f_send.at[k, side])

    @pl.loop(0, K2)
    def _(m):
        done(out2.at[m, :, pl.ds(0, PLANE - 1)], a2_send.at[m])


def return_kernel(
    k1, hid, gpk, wd_hbm, out,
    wd, y1, y2, s1, s2, r1, l1, l2, t1, e1, t2, e2, u2, v1, v2,
    w_sem, s1_send, s1_recv, s2_send, s2_recv, a1_send, a1_recv, e1_send, e1_recv,
    a2_send, a2_recv, e2_send, e2_recv, v1_send, v1_recv, v2_send, v2_recv,
):
    me = Place()
    half = TOK // 2
    low, high = pl.ds(0, PLANE // 2), pl.ds(PLANE // 2, PLANE // 2)
    across = lax.rem(me.z + 2, NZ)
    own_rows = pl.ds(pl.multiple_of(me.c * TOK, TOK), TOK)
    core_rows = pl.ds(pl.multiple_of((1 - me.c) * TOK, TOK), TOK)
    for kk in range(k1 + K2):
        pltpu.make_async_copy(wd_hbm.at[:, pl.ds(kk * CW, CW)], wd.at[kk], w_sem.at[kk]).start()
    enter([me.plane(off)[1] for off in OFFS] + [me.core, me.z_up, me.z_down])

    def down(to, kk):
        done(wd.at[kk], w_sem.at[kk])

        @pl.loop(0, CW // 256)
        def _(n):
            cols = pl.ds(pl.multiple_of(n * 256, 256), 256)
            part = jnp.dot(hid[...], wd[kk, :, cols], preferred_element_type=F32)
            to[:, :, :, cols] = part.astype(BF16).reshape(NZ, PLANE, 2 * CAP, 256)

    def plus(a, b):
        return (a.astype(F32) + b.astype(F32)).astype(BF16)

    def first(k):
        down(y1.at[k], k)
        send(y1.at[k, across, low], s1.at[k, 0], s1_send.at[k, 0], s1_recv.at[k, 0], me.z_up)
        send(y1.at[k, across, high], s1.at[k, 1], s1_send.at[k, 1], s1_recv.at[k, 1], me.z_down)

    def second(k):
        done(s1.at[k, 0], s1_recv.at[k, 0])
        y1[k, me.up, low] = plus(y1[k, me.up, low], s1[k, 0])
        send(y1.at[k, me.up], s2.at[k, 0], s2_send.at[k, 0], s2_recv.at[k, 0], me.z_up)
        done(s1.at[k, 1], s1_recv.at[k, 1])
        y1[k, me.down, high] = plus(y1[k, me.down, high], s1[k, 1])
        send(y1.at[k, me.down], s2.at[k, 1], s2_send.at[k, 1], s2_recv.at[k, 1], me.z_down)

    def third(k):
        done(s2.at[k, 0], s2_recv.at[k, 0])
        done(s2.at[k, 1], s2_recv.at[k, 1])
        r1[k] = (y1[k, me.z].astype(F32) + s2[k, 0].astype(F32) + s2[k, 1].astype(F32)).astype(BF16)
        here = l1.at[k, me.j]
        for off in OFFS:
            j, device = me.plane(off)
            send(r1.at[k, j], here, a1_send.at[k], a1_recv.at[k], device)
        pltpu.make_async_copy(r1.at[k, me.j], here, a1_recv.at[k]).start()

    def combine(zz, rows):
        rows = rows.reshape(2 * PLANE * CAP, CW)
        return jnp.dot(gpk[zz, 0], rows, preferred_element_type=F32) + jnp.dot(
            gpk[zz, 1], rows, preferred_element_type=F32
        )

    def fourth(k):
        done(l1.at[k], a1_recv.at[k])
        t1[k] = combine(me.z, l1[k])
        send(t1.at[k, core_rows], e1.at[k], e1_send.at[k], e1_recv.at[k], me.core)

    def fifth(k):
        done(e1.at[k], e1_recv.at[k])
        out[:, pl.ds(pl.multiple_of(k * CW, CW), CW)] = (t1[k, own_rows] + e1[k]).astype(BF16)

    def other_first(m):
        down(y2.at[m], k1 + m)
        here = l2.at[m, :, me.j]
        for off in OFFS:
            j, device = me.plane(off)
            send(y2.at[m, :, j], here, a2_send.at[m], a2_recv.at[m], device)
        pltpu.make_async_copy(y2.at[m, :, me.j], here, a2_recv.at[m]).start()

    def other_second(m):
        done(l2.at[m], a2_recv.at[m])

        @pl.loop(0, NZ)
        def _(zz):
            t2[m, zz] = combine(zz, l2[m, zz])

        send(t2.at[m, :, core_rows], e2.at[m], e2_send.at[m], e2_recv.at[m], me.core)

    def other_third(m):
        done(e2.at[m], e2_recv.at[m])
        for zz in range(NZ):
            u2[m, zz] = (t2[m, zz, own_rows] + e2[m, zz]).astype(BF16)
        send(u2.at[m, across, pl.ds(0, half)], v1.at[m, 0], v1_send.at[m, 0], v1_recv.at[m, 0], me.z_up)
        send(u2.at[m, across, pl.ds(half, half)], v1.at[m, 1], v1_send.at[m, 1], v1_recv.at[m, 1], me.z_down)

    def other_fourth(m):
        done(v1.at[m, 0], v1_recv.at[m, 0])
        u2[m, me.up, :half] = plus(u2[m, me.up, :half], v1[m, 0])
        send(u2.at[m, me.up], v2.at[m, 0], v2_send.at[m, 0], v2_recv.at[m, 0], me.z_up)
        done(v1.at[m, 1], v1_recv.at[m, 1])
        u2[m, me.down, half:] = plus(u2[m, me.down, half:], v1[m, 1])
        send(u2.at[m, me.down], v2.at[m, 1], v2_send.at[m, 1], v2_recv.at[m, 1], me.z_down)

    def other_fifth(m):
        done(v2.at[m, 0], v2_recv.at[m, 0])
        done(v2.at[m, 1], v2_recv.at[m, 1])
        total = u2[m, me.z].astype(F32) + v2[m, 0].astype(F32) + v2[m, 1].astype(F32)
        out[:, pl.ds(pl.multiple_of((k1 + m) * CW, CW), CW)] = total.astype(BF16)

    def between(k, lag, count, step):
        @pl.when((k >= lag) & (k < lag + count))
        def _():
            step(k - lag)

    def every_second(k, lag, step):
        @pl.when((k >= lag) & ((k - lag) % 2 == 0) & ((k - lag) // 2 < K2))
        def _():
            step((k - lag) // 2)

    @pl.loop(0, k1 + 5)
    def _(k):
        between(k, 0, k1, first)
        between(k, 0, K2, other_first)
        between(k, 1, k1, second)
        between(k, 2, k1, third)
        between(k, 3, k1, fourth)
        between(k, 4, k1, fifth)
        every_second(k, 3, other_second)
        every_second(k, 4, other_third)
        every_second(k, 5, other_fourth)
        every_second(k, 6, other_fifth)

    @pl.loop(0, k1)
    def _(k):
        for side in range(2):
            done(s1.at[k, 0], s1_send.at[k, side])
            done(s2.at[k, 0], s2_send.at[k, side])
        done(r1.at[k, pl.ds(0, PLANE - 1)], a1_send.at[k])
        done(e1.at[k], e1_send.at[k])

    @pl.loop(0, K2)
    def _(m):
        done(y2.at[m, :, pl.ds(0, PLANE - 1)], a2_send.at[m])
        done(e2.at[m], e2_send.at[m])
        for side in range(2):
            done(v1.at[m, 0], v1_send.at[m, side])
            done(v2.at[m, 0], v2_send.at[m, side])


def on_device(tokens, routes, gates, w_gate, w_up, w_down):
    width = tokens.shape[1]
    k1 = width // CW - K2
    hid_cols = w_gate.shape[2]
    rows = NZ * PLANE * 2 * CAP
    experts = 2 * PLANE
    flat = routes.reshape(-1)
    onehot = (flat[:, None] == jnp.arange(experts)[None, :]).astype(jnp.int32)
    before = jnp.cumsum(onehot, axis=0) - onehot
    slot = jnp.sum(before * onehot, axis=1)
    target = (flat * CAP + slot).reshape(routes.shape).astype(F32)
    meta = jnp.concatenate([target, gates], axis=1).T
    core = lax.axis_index("rep") % 2
    lane_core = lax.broadcasted_iota(jnp.int32, (4, 2 * TOK), 1) // TOK
    meta = jnp.where(lane_core == core, jnp.concatenate([meta, meta], axis=1), 0.0)
    meta = jnp.concatenate([meta, jnp.zeros((4, 2 * TOK), F32)], axis=0)

    dma = pltpu.SemaphoreType.DMA
    vmem = pl.BlockSpec(memory_space=pltpu.VMEM)
    hbm = pl.BlockSpec(memory_space=pl.ANY)
    slots = 2 * CAP
    hid, gpk = pl.pallas_call(
        functools.partial(dispatch_kernel, k1),
        out_shape=(
            jax.ShapeDtypeStruct((rows, hid_cols), BF16),
            jax.ShapeDtypeStruct((NZ, 2, 2 * TOK, PLANE * slots), BF16),
        ),
        in_specs=[vmem, vmem, hbm, hbm],
        out_specs=(vmem, vmem),
        scratch_shapes=[
            pltpu.VMEM((k1, 2 * TOK, CW), BF16),
            pltpu.VMEM((NZ, 2 * TOK, K2 * CW), BF16),
            pltpu.VMEM((NZ, 2, 8, 2 * TOK), F32),
            pltpu.VMEM((NZ, PLANE * slots, 2 * TOK), BF16),
            pltpu.VMEM((k1, PLANE, slots, CW), BF16),
            pltpu.VMEM((K2, NZ, PLANE, slots, CW), BF16),
            pltpu.VMEM((k1, NZ, PLANE, slots, CW), BF16),
            pltpu.VMEM((K2, NZ, PLANE, slots, CW), BF16),
            pltpu.VMEM((width, hid_cols), BF16),
            pltpu.VMEM((width, hid_cols), BF16),
            pltpu.VMEM((rows, 2 * hid_cols), F32),
            dma((2, k1 + K2)), dma((2 * NZ - 1,)), dma, dma((k1,)), dma((k1,)), dma((4,)), dma((5,)), dma, dma,
            dma((k1,)), dma((k1,)), dma((k1, 2)), dma((k1, 2)), dma((k1, 2)), dma((k1, 2)), dma((K2,)), dma((K2,)),
        ],
        compiler_params=pltpu.CompilerParams(collective_id=0, has_side_effects=True, vmem_limit_bytes=60 << 20),
    )(tokens, meta, w_gate[0], w_up[0])

    return pl.pallas_call(
        functools.partial(return_kernel, k1),
        out_shape=jax.ShapeDtypeStruct(tokens.shape, BF16),
        in_specs=[vmem, vmem, hbm],
        out_specs=vmem,
        scratch_shapes=[
            pltpu.VMEM((k1 + K2, hid_cols, CW), BF16),
            pltpu.VMEM((k1, NZ, PLANE, slots, CW), BF16),
            pltpu.VMEM((K2, NZ, PLANE, slots, CW), BF16),
            pltpu.VMEM((k1, 2, PLANE // 2, slots, CW), BF16),
            pltpu.VMEM((k1, 2, PLANE, slots, CW), BF16),
            pltpu.VMEM((k1, PLANE, slots, CW), BF16),
            pltpu.VMEM((k1, PLANE, slots, CW), BF16),
            pltpu.VMEM((K2, NZ, PLANE, slots, CW), BF16),
            pltpu.VMEM((k1, 2 * TOK, CW), F32),
            pltpu.VMEM((k1, TOK, CW), F32),
            pltpu.VMEM((K2, NZ, 2 * TOK, CW), F32),
            pltpu.VMEM((K2, NZ, TOK, CW), F32),
            pltpu.VMEM((K2, NZ, TOK, CW), BF16),
            pltpu.VMEM((K2, 2, TOK // 2, CW), BF16),
            pltpu.VMEM((K2, 2, TOK, CW), BF16),
            dma((k1 + K2,)), dma((k1, 2)), dma((k1, 2)), dma((k1, 2)), dma((k1, 2)),
            dma((k1,)), dma((k1,)), dma((k1,)), dma((k1,)),
            dma((K2,)), dma((K2,)), dma((K2,)), dma((K2,)), dma((K2, 2)), dma((K2, 2)), dma((K2, 2)), dma((K2, 2)),
        ],
        compiler_params=pltpu.CompilerParams(collective_id=1, has_side_effects=True, vmem_limit_bytes=60 << 20),
    )(hid, gpk, w_down[0])


def solution(mesh):
    placed = (
        P(("rep", "head", "side"), None),
        P(("rep", "head", "side"), None),
        P(("rep", "head", "side"), None),
        P(("rep", "head"), None, "side"),
        P(("rep", "head"), None, "side"),
        P(("rep", "head"), "side", None),
    )
    return jax.shard_map(
        on_device,
        mesh=mesh,
        in_specs=placed,
        out_specs=P(("rep", "head", "side"), None),
        check_vma=False,
    )
```

time: 436 us -> 256 us (0.59)
  waiting for transfers between devices: 268 us -> 0 us
  Pallas kernels: 0 us -> 250 us
  blocking collectives: 106 us -> 0 us
  matrix products: 37.8 us -> 0 us
  between operations: 13.5 us -> 0.05 us
  local copies, waits for them, and re-layouts: 9.07 us -> 3.88 us
    pallas_call x0 -> x2, Pallas kernels: none -> 250 us  [the longest x1 134 us: on_device(): pl.pallas_call(functools.partial(return_kernel, k1), out_shape=jax.ShapeD...]
    all_gather x1 -> x0, waiting for transfers between devices: 135 us -> none  [on_device(): rows_all = lax.all_gather(arrived, 'side', axis=0, tiled=True)]
    reduce_scatter x1 -> x0, waiting for transfers between devices: 133 us -> none  [on_device(): lax.psum_scatter(jnp.einsum('gech,ehd->gecd', hidden, w_down, preferred_e...]
    all_to_all x2 -> x0, blocking collectives: 106 us -> none  [the longest x1 53.4 us: on_device(): lax.all_to_all(outgoing, ('rep', 'head'), split_axis=0, concat_axis=0, ti...]
    dot_general x5 -> x0, matrix products: 37.8 us -> none  [the longest x1 13.2 us: on_device(): jnp.einsum('gecd,edh->gech', rows_all, w_up, preferred_element_type=jnp.f...]
  transfers between devices with their start and end apart: 2 -> 0, of which waited for: 2 -> 0; matrix products, arithmetic and copies ran while one was open for 0% -> 0% of each run, Pallas kernels for 0% -> 0%
where the time goes in v1:
time: 256 us
  Pallas kernels  250 us (98%)
  local copies, waits for them, and re-layouts  3.88 us (2%)
    pallas_call x1, Pallas kernels, on_device(): pl.pallas_call(functools.partial(return_kernel, k1), out_shape=jax.ShapeD...  134 us
    pallas_call x1, Pallas kernels, on_device(): pl.pallas_call(functools.partial(dispatch_kernel, k1), out_shape=(jax.Sha...  116 us

profile of v1, /device:TPU:1, one launch (start us, length us, event | category | flops | bytes accessed | tf_op | source)
XLA Modules:
  0.0 256.0 jit_solution(10450010241378824631)
XLA Ops:
  0.0 0.8 copy.9
  0.8 0.1 eq.25
  0.9 0.1 fusion
  1.0 0.2 reduce_window_sum.11
  1.2 0.2 select_reduce_fusion
  1.4 0.1 reduce_sum.12
  1.5 0.1 copy.10
  1.6 0.7 add_convert_fusion
  2.3 0.7 maximum_bitcast_fusion
  3.0 0.1 maximum_select_fusion
  3.1 0.6 concatenate.11.meta
  3.7 116.4 %shard_map.64 = (bf16[1024,512]{1,0:T(8,128)(2,1)}, bf16[4,2,128,256]{3,2,1,0:T(8,128)(2,1)}) custom-call(bf16[64,7168]{1,0:T(8,128)(2,1)} %tok.1, f32[8,128]{1,0:T(8,128)} %concatenate.11.meta, bf16[7168,512]{1,0:T(8,128)(2,1)} %bitcast.6, bf16[7168,512]{1,0:T(8,128)(2,1)} %bitcast.7), custom_call_target="tpu_custom_call" | custom-call | tf_op jit(solution)/shard_map/pallas_call | solution.py:414
  120.0 133.8 %shard_map.65 = bf16[64,7168]{1,0:T(8,128)(2,1)} custom-call(bf16[1024,512]{1,0:T(8,128)(2,1)} %get-tuple-element.7.hid, bf16[4,2,128,256]{3,2,1,0:T(8,128)(2,1)} %get-tuple-element.8.gpk, bf16[512,7168]{1,0:T(8,128)(2,1)} %bitcast.5), custom_call_target="tpu_custom_call" | custom-call | tf_op jit(solution)/shard_map/pallas_call | solution.py:440
  253.9 2.2 copy.12
  (2 shorter events, 0.0 us)

commit v2 on v1

v2 whole, which is shorter than its diff:
```python
import functools

import jax
import jax.numpy as jnp
from jax import lax
from jax.experimental import pallas as pl
from jax.experimental.pallas import tpu as pltpu
from jax.sharding import PartitionSpec as P

MESH = pl.DeviceIdType.MESH
F32, BF16 = jnp.float32, jnp.bfloat16
CW = 512
K2 = 5
SLOTS1, SLOTS2 = 3, 2
CAP = 8
TOK = 64
NX, NY, NZ = 4, 4, 4
PLANE = NX * NY
OFFS = sorted(
    [(dx, dy) for dx in range(NX) for dy in range(NY) if (dx, dy) != (0, 0)],
    key=lambda off: min(off[0], NX - off[0]) + min(off[1], NY - off[1]),
)


class Place:
    def __init__(self):
        rep = lax.axis_index("rep")
        self.x, self.c = rep // 2, rep % 2
        self.y, self.z = lax.axis_index("head"), lax.axis_index("side")
        self.j = self.x * NY + self.y
        self.up, self.down = lax.rem(self.z + 1, NZ), lax.rem(self.z + NZ - 1, NZ)
        self.core = self.dev(self.x, 1 - self.c, self.y, self.z)
        self.z_up = self.dev(self.x, self.c, self.y, self.up)
        self.z_down = self.dev(self.x, self.c, self.y, self.down)

    def dev(self, x, c, y, z):
        return (x * 2 + c, y, z)

    def plane(self, off):
        x, y = lax.rem(self.x + off[0], NX), lax.rem(self.y + off[1], NY)
        return x * NY + y, self.dev(x, self.c, y, self.z)

    def column(self):
        own = []
        for dc in range(2):
            for dz in range(NZ):
                if (dc, dz) != (0, 0):
                    own.append(self.dev(self.x, lax.rem(self.c + dc, 2), self.y, lax.rem(self.z + dz, NZ)))
        return own


def enter(partners):
    barrier = pltpu.get_barrier_semaphore()
    for device in partners:
        pl.semaphore_signal(barrier, inc=1, device_id=device, device_id_type=MESH)
    pl.semaphore_wait(barrier, len(partners))


def send(src, dst, send_sem, recv_sem, device):
    pltpu.make_async_remote_copy(
        src_ref=src, dst_ref=dst, send_sem=send_sem, recv_sem=recv_sem, device_id=device, device_id_type=MESH
    ).start()


def done(ref, sem):
    pltpu.make_async_copy(ref, ref, sem).wait()


def kernel(
    k1, tok, routes, gates, wg_hbm, wu_hbm, wd_hbm, out,
    meta, metas, tokc, ztok, pk, gpk, out1, out2, x1, x2, w1, w2, acc, hid,
    s1, s2, l1, l2, e1, e2, u2, v1, v2,
    w1_sem, w2_sem, m_send, m_recv, c_send, c_recv, t_send, t_recv, tc_send, tc_recv,
    a1_send, a1_recv, z_send, z_recv, f_send, f_recv, a2_send, a2_recv,
    s1_send, s1_recv, s2_send, s2_recv, b1_send, b1_recv, e1_send, e1_recv,
    b2_send, b2_recv, e2_send, e2_recv, v1_send, v1_recv, v2_send, v2_recv,
):
    y1, y2, r1, t1, t2 = x1, x2, out1, tokc, ztok
    me = Place()
    d1 = k1 * CW
    half = TOK // 2
    low, high = pl.ds(0, PLANE // 2), pl.ds(PLANE // 2, PLANE // 2)
    across = lax.rem(me.z + 2, NZ)
    own_rows = pl.ds(pl.multiple_of(me.c * TOK, TOK), TOK)
    core_rows = pl.ds(pl.multiple_of((1 - me.c) * TOK, TOK), TOK)

    def load_in(w, sem, slot, kk):
        rows = pl.ds(pl.multiple_of(kk * CW, CW), CW)
        pltpu.make_async_copy(wg_hbm.at[rows], w.at[slot, 0], sem.at[slot, 0]).start()
        pltpu.make_async_copy(wu_hbm.at[rows], w.at[slot, 1], sem.at[slot, 1]).start()

    def load_down(w, sem, slot, kk):
        cols = pl.ds(pl.multiple_of(kk * CW, CW), CW)
        pltpu.make_async_copy(wd_hbm.at[:, cols], w.at[slot, 0], sem.at[slot, 0]).start()

    for k in range(SLOTS1):
        load_in(w1, w1_sem, k, k)
    for m in range(SLOTS2):
        load_in(w2, w2_sem, m, k1 + m)
    experts = 2 * PLANE
    expert = lax.broadcasted_iota(jnp.int32, (experts, TOK), 0)
    named = [jnp.where(expert == routes[i:i + 1, :], 1.0, 0.0) for i in range(2)]
    earlier = lax.broadcasted_iota(jnp.int32, (TOK, TOK), 0) < lax.broadcasted_iota(jnp.int32, (TOK, TOK), 1)
    before = jnp.dot((named[0] + named[1]).astype(BF16), jnp.where(earlier, 1.0, 0.0).astype(BF16), preferred_element_type=F32)
    parts = []
    for i in range(2):
        slot = jnp.sum(before * named[i], axis=0, keepdims=True)
        parts.append(routes[i:i + 1, :].astype(F32) * CAP + slot)
    parts += [gates[0:1, :], gates[1:2, :], jnp.zeros((4, TOK), F32)]
    own = jnp.concatenate(parts, axis=0)
    lane_core = lax.broadcasted_iota(jnp.int32, (8, 2 * TOK), 1) // TOK
    meta[...] = jnp.where(lane_core == me.c, jnp.concatenate([own, own], axis=1), 0.0)
    enter([me.plane(off)[1] for off in OFFS] + me.column())

    own_meta = metas.at[me.z, me.c]
    pltpu.make_async_copy(meta, own_meta, m_recv).start()
    for i, device in enumerate(me.column()):
        send(meta, own_meta, m_send.at[i], m_recv, device)
    tail = pl.ds(d1, K2 * CW)
    own_tok = ztok.at[me.z, own_rows]
    send(tok.at[:, tail], own_tok, t_send.at[0], t_recv.at[0], me.z_up)
    send(tok.at[:, tail], own_tok, t_send.at[1], t_recv.at[1], me.z_down)
    for k in range(k1):
        cols = pl.ds(k * CW, CW)
        send(tok.at[:, cols], tokc.at[k, own_rows], c_send.at[k], c_recv.at[k], me.core)
        pltpu.make_async_copy(tok.at[:, cols], tokc.at[k, own_rows], c_recv.at[k]).start()
    pltpu.make_async_copy(tok.at[:, tail], own_tok, t_recv.at[4]).start()

    def hits(zz):
        shape = (2 * PLANE * CAP, 2 * TOK)
        row = lax.broadcasted_iota(jnp.int32, shape, 0)
        col = lax.broadcasted_iota(jnp.int32, shape, 1)
        dest = row // (2 * CAP)
        want = ((2 * (dest // NY) + me.c) * NY + dest % NY) * CAP + row % CAP
        want = jnp.where((row // CAP) % 2 == col // TOK, want, -1).astype(F32)
        both = metas[zz, 0] + metas[zz, 1]
        return both, want == both[0:1], want == both[1:2]

    def pickers(zz):
        _, hit0, hit1 = hits(zz)
        pk[zz] = jnp.where(hit0 | hit1, 1.0, 0.0).astype(BF16)

    def gated_pickers(zz):
        both, hit0, hit1 = hits(zz)
        gated = jnp.where(hit0, both[2:3], 0.0) + jnp.where(hit1, both[3:4], 0.0)
        gated = gated.T
        high = gated.astype(BF16)
        gpk[zz, 0] = high
        gpk[zz, 1] = (gated - high.astype(F32)).astype(BF16)

    done(metas, m_recv)
    pickers(me.z)

    def p1_issue(k):
        done(tokc.at[k], c_recv.at[k])
        picked = jnp.dot(pk[me.z], tokc[k], preferred_element_type=F32)
        out1[k] = picked.astype(BF16).reshape(PLANE, 2 * CAP, CW)
        here = x1.at[k, me.z, me.j]
        for off in OFFS:
            j, device = me.plane(off)
            send(out1.at[k, j], here, a1_send.at[k], a1_recv.at[k], device)
        pltpu.make_async_copy(out1.at[k, me.j], here, a1_recv.at[k]).start()

    def z_issue(k):
        block = x1.at[k, me.z]
        done(block, a1_recv.at[k])
        send(block, block, z_send.at[k, 0], z_recv.at[k, 0], me.z_up)
        send(block, block, z_send.at[k, 1], z_recv.at[k, 1], me.z_down)

    def z_forward(k):
        done(x1.at[k, me.down], z_recv.at[k, 0])
        part = x1.at[k, me.down, low]
        send(part, part, f_send.at[k, 0], f_recv.at[k, 0], me.z_up)
        done(x1.at[k, me.up], z_recv.at[k, 1])
        part = x1.at[k, me.up, high]
        send(part, part, f_send.at[k, 1], f_recv.at[k, 1], me.z_down)

    def project(block, w, sem, slot):
        hid_cols = hid.shape[1]
        for i in range(2):
            done(w.at[slot, i], sem.at[slot, i])

            @pl.loop(0, hid_cols // 256)
            def _(n):
                cols = pl.ds(pl.multiple_of(n * 256, 256), 256)
                to = pl.ds(pl.multiple_of(i * hid_cols + n * 256, 256), 256)
                part = jnp.dot(block[...].reshape(acc.shape[0], CW), w[slot, i, :, cols], preferred_element_type=F32)
                acc[:, to] = acc[:, to] + part

    def refill(w, sem, n, slots, count, base):
        slot = lax.rem(n, slots)

        @pl.when(n + slots < count)
        def _():
            load_in(w, sem, slot, base + n + slots)

        @pl.when(n + slots >= count)
        def _():
            load_down(w, sem, slot, base + slot)

    def mm1(k):
        done(x1.at[k, across, pl.ds(0, PLANE // 2)], f_recv.at[k, 0])
        done(x1.at[k, across, pl.ds(PLANE // 2, PLANE // 2)], f_recv.at[k, 1])
        project(x1.at[k], w1, w1_sem, lax.rem(k, SLOTS1))
        refill(w1, w1_sem, k, SLOTS1, k1, 0)

    def p2_issue(m):
        cols = pl.ds(pl.multiple_of(m * CW, CW), CW)

        @pl.loop(0, NZ)
        def _(zz):
            picked = jnp.dot(pk[zz], ztok[zz, :, cols], preferred_element_type=F32)
            out2[m, zz] = picked.astype(BF16).reshape(PLANE, 2 * CAP, CW)

        here = x2.at[m, :, me.j]
        for off in OFFS:
            j, device = me.plane(off)
            send(out2.at[m, :, j], here, a2_send.at[m], a2_recv.at[m], device)
        pltpu.make_async_copy(out2.at[m, :, me.j], here, a2_recv.at[m]).start()

    def mm2(m):
        done(x2.at[m], a2_recv.at[m])
        project(x2.at[m], w2, w2_sem, lax.rem(m, SLOTS2))
        refill(w2, w2_sem, m, SLOTS2, K2, k1)

    p1_issue(0)
    p1_issue(1)
    p1_issue(2)
    done(ztok.at[me.down, own_rows], t_recv.at[0])
    part = ztok.at[me.down, pl.ds(pl.multiple_of(me.c * TOK, TOK), half)]
    send(part, part, t_send.at[2], t_recv.at[2], me.z_up)
    done(ztok.at[me.up, own_rows], t_recv.at[1])
    part = ztok.at[me.up, pl.ds(pl.multiple_of(me.c * TOK + half, half), half)]
    send(part, part, t_send.at[3], t_recv.at[3], me.z_down)
    z_issue(0)
    p1_issue(3)
    for dz in range(1, NZ):
        pickers(lax.rem(me.z + dz, NZ))
    z_issue(1)
    done(ztok.at[across, pl.ds(pl.multiple_of(me.c * TOK, TOK), half)], t_recv.at[2])
    done(ztok.at[across, pl.ds(pl.multiple_of(me.c * TOK + half, half), half)], t_recv.at[3])
    done(own_tok, t_recv.at[4])
    mine = ztok.at[:, own_rows]
    send(mine, mine, tc_send, tc_recv, me.core)
    acc[...] = jnp.zeros_like(acc)
    other = ztok.at[:, pl.ds(pl.multiple_of((1 - me.c) * TOK, TOK), TOK)]
    done(other, tc_recv)

    def between(k, lag, count, step):
        @pl.when((k >= lag) & (k < lag + count))
        def _():
            step(k - lag)

    def every_second(k, lag, step):
        @pl.when((k >= lag) & ((k - lag) % 2 == 0) & ((k - lag) // 2 < K2))
        def _():
            step((k - lag) // 2)

    @pl.loop(0, max(k1 + 2, 2 + 2 * K2))
    def _(k):
        @pl.when((k >= 2) & (k < k1))
        def _():
            z_issue(k)

        between(k, 1, k1, z_forward)

        @pl.when(k + 4 < k1)
        def _():
            p1_issue(k + 4)

        every_second(k, 0, p2_issue)
        between(k, 2, NZ, gated_pickers)
        between(k, 2, k1, mm1)
        every_second(k, 3, mm2)

    @pl.loop(0, acc.shape[0] // 128)
    def _(i):
        rows = pl.ds(pl.multiple_of(i * 128, 128), 128)
        hc = hid.shape[1]
        g, u = acc[rows, :hc], acc[rows, hc:]
        hid[rows, :] = (g / (1.0 + jnp.exp(-g)) * u).astype(BF16)

    for i in range(2 * NZ - 1):
        done(meta, m_send.at[i])
    done(tok.at[:, tail], t_send.at[0])
    done(tok.at[:, tail], t_send.at[1])
    done(ztok.at[0, pl.ds(0, half)], t_send.at[2])
    done(ztok.at[0, pl.ds(0, half)], t_send.at[3])
    done(mine, tc_send)

    def left_z(k):
        for side in range(2):
            done(x1.at[k, 0], z_send.at[k, side])
            done(x1.at[k, 0, low], f_send.at[k, side])

    def left_plane(k):
        done(tokc.at[k, pl.ds(0, TOK)], c_send.at[k])
        done(out1.at[k, pl.ds(0, PLANE - 1)], a1_send.at[k])

    def left_tokens(m):
        done(out2.at[m, :, pl.ds(0, PLANE - 1)], a2_send.at[m])

    def down(to, w, sem, n, slots, count, base):
        slot = lax.rem(n, slots)
        done(w.at[slot, 0], sem.at[slot, 0])

        @pl.loop(0, CW // 256)
        def _(i):
            cols = pl.ds(pl.multiple_of(i * 256, 256), 256)
            part = jnp.dot(hid[...], w[slot, 0, :, cols], preferred_element_type=F32)
            to[:, :, :, cols] = part.astype(BF16).reshape(NZ, PLANE, 2 * CAP, 256)

        @pl.when(n + slots < count)
        def _():
            load_down(w, sem, slot, base + n + slots)

    def plus(a, b):
        return (a.astype(F32) + b.astype(F32)).astype(BF16)

    def first(k):
        left_z(k)
        down(y1.at[k], w1, w1_sem, k, SLOTS1, k1, 0)
        send(y1.at[k, across, low], s1.at[k, 0], s1_send.at[k, 0], s1_recv.at[k, 0], me.z_up)
        send(y1.at[k, across, high], s1.at[k, 1], s1_send.at[k, 1], s1_recv.at[k, 1], me.z_down)

    def second(k):
        done(s1.at[k, 0], s1_recv.at[k, 0])
        y1[k, me.up, low] = plus(y1[k, me.up, low], s1[k, 0])
        send(y1.at[k, me.up], s2.at[k, 0], s2_send.at[k, 0], s2_recv.at[k, 0], me.z_up)
        done(s1.at[k, 1], s1_recv.at[k, 1])
        y1[k, me.down, high] = plus(y1[k, me.down, high], s1[k, 1])
        send(y1.at[k, me.down], s2.at[k, 1], s2_send.at[k, 1], s2_recv.at[k, 1], me.z_down)

    def third(k):
        done(s2.at[k, 0], s2_recv.at[k, 0])
        done(s2.at[k, 1], s2_recv.at[k, 1])
        left_plane(k)
        r1[k] = (y1[k, me.z].astype(F32) + s2[k, 0].astype(F32) + s2[k, 1].astype(F32)).astype(BF16)
        here = l1.at[k, me.j]
        for off in OFFS:
            j, device = me.plane(off)
            send(r1.at[k, j], here, b1_send.at[k], b1_recv.at[k], device)
        pltpu.make_async_copy(r1.at[k, me.j], here, b1_recv.at[k]).start()

    def combine(zz, rows):
        rows = rows.reshape(2 * PLANE * CAP, CW)
        return jnp.dot(gpk[zz, 0], rows, preferred_element_type=F32) + jnp.dot(
            gpk[zz, 1], rows, preferred_element_type=F32
        )

    def fourth(k):
        done(l1.at[k], b1_recv.at[k])
        t1[k] = combine(me.z, l1[k]).astype(BF16)
        send(t1.at[k, core_rows], e1.at[k], e1_send.at[k], e1_recv.at[k], me.core)

    def fifth(k):
        done(e1.at[k], e1_recv.at[k])
        out[:, pl.ds(pl.multiple_of(k * CW, CW), CW)] = plus(t1[k, own_rows], e1[k])

    def other_first(m):
        left_tokens(m)
        down(y2.at[m], w2, w2_sem, m, SLOTS2, K2, k1)
        here = l2.at[m, :, me.j]
        for off in OFFS:
            j, device = me.plane(off)
            send(y2.at[m, :, j], here, b2_send.at[m], b2_recv.at[m], device)
        pltpu.make_async_copy(y2.at[m, :, me.j], here, b2_recv.at[m]).start()

    def other_second(m):
        done(l2.at[m], b2_recv.at[m])

        @pl.loop(0, NZ)
        def _(zz):
            t2[zz, :, pl.ds(pl.multiple_of(m * CW, CW), CW)] = combine(zz, l2[m, zz]).astype(BF16)

        send(t2.at[:, core_rows, pl.ds(pl.multiple_of(m * CW, CW), CW)], e2.at[m], e2_send.at[m], e2_recv.at[m], me.core)

    def other_third(m):
        done(e2.at[m], e2_recv.at[m])
        for zz in range(NZ):
            u2[m, zz] = plus(t2[zz, own_rows, pl.ds(pl.multiple_of(m * CW, CW), CW)], e2[m, zz])
        send(u2.at[m, across, pl.ds(0, half)], v1.at[m, 0], v1_send.at[m, 0], v1_recv.at[m, 0], me.z_up)
        send(u2.at[m, across, pl.ds(half, half)], v1.at[m, 1], v1_send.at[m, 1], v1_recv.at[m, 1], me.z_down)

    def other_fourth(m):
        done(v1.at[m, 0], v1_recv.at[m, 0])
        u2[m, me.up, :half] = plus(u2[m, me.up, :half], v1[m, 0])
        send(u2.at[m, me.up], v2.at[m, 0], v2_send.at[m, 0], v2_recv.at[m, 0], me.z_up)
        done(v1.at[m, 1], v1_recv.at[m, 1])
        u2[m, me.down, half:] = plus(u2[m, me.down, half:], v1[m, 1])
        send(u2.at[m, me.down], v2.at[m, 1], v2_send.at[m, 1], v2_recv.at[m, 1], me.z_down)

    def other_fifth(m):
        done(v2.at[m, 0], v2_recv.at[m, 0])
        done(v2.at[m, 1], v2_recv.at[m, 1])
        total = u2[m, me.z].astype(F32) + v2[m, 0].astype(F32) + v2[m, 1].astype(F32)
        out[:, pl.ds(pl.multiple_of((k1 + m) * CW, CW), CW)] = total.astype(BF16)

    @pl.loop(0, max(k1 + 7, 4 + 2 * K2))
    def _(k):
        between(k, 0, k1, first)
        between(k, 2, k1, second)
        between(k, 0, K2, other_first)
        between(k, 3, k1, third)
        every_second(k, 2, other_second)
        every_second(k, 3, other_third)
        every_second(k, 4, other_fourth)
        every_second(k, 5, other_fifth)
        between(k, 6, k1, fourth)
        between(k, 7, k1, fifth)

    @pl.loop(0, k1)
    def _(k):
        for side in range(2):
            done(s1.at[k, 0], s1_send.at[k, side])
            done(s2.at[k, 0], s2_send.at[k, side])
        done(r1.at[k, pl.ds(0, PLANE - 1)], b1_send.at[k])
        done(e1.at[k], e1_send.at[k])

    @pl.loop(0, K2)
    def _(m):
        done(y2.at[m, :, pl.ds(0, PLANE - 1)], b2_send.at[m])
        done(e2.at[m], e2_send.at[m])
        for side in range(2):
            done(v1.at[m, 0], v1_send.at[m, side])
            done(v2.at[m, 0], v2_send.at[m, side])


def on_device(tokens, routes, gates, w_gate, w_up, w_down):
    width = tokens.shape[1]
    k1 = width // CW - K2
    hid_cols = w_gate.shape[2]
    rows = NZ * PLANE * 2 * CAP
    slots = 2 * CAP

    def dma(*shape):
        return pltpu.SemaphoreType.DMA(shape)

    vmem = pl.BlockSpec(memory_space=pltpu.VMEM)
    hbm = pl.BlockSpec(memory_space=pl.ANY)
    return pl.pallas_call(
        functools.partial(kernel, k1),
        out_shape=jax.ShapeDtypeStruct(tokens.shape, BF16),
        in_specs=[vmem, vmem, vmem, hbm, hbm, hbm],
        out_specs=vmem,
        scratch_shapes=[
            pltpu.VMEM((8, 2 * TOK), F32),
            pltpu.VMEM((NZ, 2, 8, 2 * TOK), F32),
            pltpu.VMEM((k1, 2 * TOK, CW), BF16),
            pltpu.VMEM((NZ, 2 * TOK, K2 * CW), BF16),
            pltpu.VMEM((NZ, PLANE * slots, 2 * TOK), BF16),
            pltpu.VMEM((NZ, 2, 2 * TOK, PLANE * slots), BF16),
            pltpu.VMEM((k1, PLANE, slots, CW), BF16),
            pltpu.VMEM((K2, NZ, PLANE, slots, CW), BF16),
            pltpu.VMEM((k1, NZ, PLANE, slots, CW), BF16),
            pltpu.VMEM((K2, NZ, PLANE, slots, CW), BF16),
            pltpu.VMEM((SLOTS1, 2, CW, hid_cols), BF16),
            pltpu.VMEM((SLOTS2, 2, CW, hid_cols), BF16),
            pltpu.VMEM((rows, 2 * hid_cols), F32),
            pltpu.VMEM((rows, hid_cols), BF16),
            pltpu.VMEM((k1, 2, PLANE // 2, slots, CW), BF16),
            pltpu.VMEM((k1, 2, PLANE, slots, CW), BF16),
            pltpu.VMEM((k1, PLANE, slots, CW), BF16),
            pltpu.VMEM((K2, NZ, PLANE, slots, CW), BF16),
            pltpu.VMEM((k1, TOK, CW), BF16),
            pltpu.VMEM((K2, NZ, TOK, CW), BF16),
            pltpu.VMEM((K2, NZ, TOK, CW), BF16),
            pltpu.VMEM((K2, 2, TOK // 2, CW), BF16),
            pltpu.VMEM((K2, 2, TOK, CW), BF16),
            dma(SLOTS1, 2), dma(SLOTS2, 2), dma(2 * NZ - 1), pltpu.SemaphoreType.DMA, dma(k1), dma(k1), dma(4), dma(5),
            pltpu.SemaphoreType.DMA, pltpu.SemaphoreType.DMA,
            dma(k1), dma(k1), dma(k1, 2), dma(k1, 2), dma(k1, 2), dma(k1, 2), dma(K2), dma(K2),
            dma(k1, 2), dma(k1, 2), dma(k1, 2), dma(k1, 2), dma(k1), dma(k1), dma(k1), dma(k1),
            dma(K2), dma(K2), dma(K2), dma(K2), dma(K2, 2), dma(K2, 2), dma(K2, 2), dma(K2, 2),
        ],
        compiler_params=pltpu.CompilerParams(collective_id=0, has_side_effects=True, vmem_limit_bytes=61 << 20),
    )(tokens, routes.T, gates.T, w_gate[0], w_up[0], w_down[0])


def solution(mesh):
    placed = (
        P(("rep", "head", "side"), None),
        P(("rep", "head", "side"), None),
        P(("rep", "head", "side"), None),
        P(("rep", "head"), None, "side"),
        P(("rep", "head"), None, "side"),
        P(("rep", "head"), "side", None),
    )
    return jax.shard_map(
        on_device,
        mesh=mesh,
        in_specs=placed,
        out_specs=P(("rep", "head", "side"), None),
        check_vma=False,
    )
```

time: 256 us -> 213 us (0.83)
  Pallas kernels: 250 us -> 209 us
    pallas_call x2 -> x1, Pallas kernels: 250 us -> 209 us  [on_device(): pl.pallas_call(functools.partial(kernel, k1), out_shape=jax.ShapeDtypeStr...]
where the time goes in v2:
time: 213 us; the launch traced here: 211 us
  Pallas kernels  209 us (98%)
  local copies, waits for them, and re-layouts  2.16 us (1%)
    pallas_call x1, Pallas kernels, on_device(): pl.pallas_call(functools.partial(kernel, k1), out_shape=jax.ShapeDtypeStr...  209 us

profile of v2, /device:TPU:1, one launch (start us, length us, event | category | flops | bytes accessed | tf_op | source)
XLA Modules:
  0.0 211.4 jit_solution(18440038102030172886)
XLA Ops:
  0.0 209.2 %shard_map.64 = bf16[64,7168]{1,0:T(8,128)(2,1)} custom-call(bf16[64,7168]{1,0:T(8,128)(2,1)} %tok.1, s32[2,64]{1,0:T(2,128)} %bitcast.8, f32[2,64]{1,0:T(2,128)} %bitcast.9, bf16[7168,512]{1,0:T(8,128)(2,1)} %bitcast.5, bf16[7168,512]{1,0:T(8,128)(2,1)} %bitcast.6, bf16[512,7168]{1,0:T(8,128)(2,1)} %bitcast.7), custom_call_target="tpu_custom_call" | custom-call | tf_op jit(solution)/shard_map/pallas_call | solution.py:441
  209.2 2.2 %copy.8 = bf16[64,7168]{1,0:T(8,128)(2,1)} copy(bf16[64,7168]{1,0:T(8,128)(2,1)} %shard_map.64) | data formatting | bytes 1835008

commit v3 on v2

--- a/solution.py
+++ b/solution.py
@@ -11,7 +11,7 @@
 F32, BF16 = jnp.float32, jnp.bfloat16
 CW = 512
 K2 = 5
-SLOTS1, SLOTS2 = 3, 2
+SLOTS1, SLOTS2 = 3, 3
 CAP = 8
 TOK = 64
 NX, NY, NZ = 4, 4, 4
@@ -251,12 +251,12 @@
         def _():
             step(k - lag)
 
-    def every_second(k, lag, step):
-        @pl.when((k >= lag) & ((k - lag) % 2 == 0) & ((k - lag) // 2 < K2))
+    def every_second(k, lag, step, count):
+        @pl.when((k >= lag) & ((k - lag) % 2 == 0) & ((k - lag) // 2 < count))
         def _():
             step((k - lag) // 2)
 
-    @pl.loop(0, max(k1 + 2, 2 + 2 * K2))
+    @pl.loop(0, max(k1 + 1, 3 + 2 * (K2 - 1)))
     def _(k):
         @pl.when((k >= 2) & (k < k1))
         def _():
@@ -268,17 +268,10 @@
         def _():
             p1_issue(k + 4)
 
-        every_second(k, 0, p2_issue)
+        every_second(k, 0, p2_issue, K2)
         between(k, 2, NZ, gated_pickers)
-        between(k, 2, k1, mm1)
-        every_second(k, 3, mm2)
-
-    @pl.loop(0, acc.shape[0] // 128)
-    def _(i):
-        rows = pl.ds(pl.multiple_of(i * 128, 128), 128)
-        hc = hid.shape[1]
-        g, u = acc[rows, :hc], acc[rows, hc:]
-        hid[rows, :] = (g / (1.0 + jnp.exp(-g)) * u).astype(BF16)
+        between(k, 2, k1 - 1, mm1)
+        every_second(k, 4, mm2, K2 - 1)
 
     for i in range(2 * NZ - 1):
         done(meta, m_send.at[i])
@@ -300,6 +293,15 @@
     def left_tokens(m):
         done(out2.at[m, :, pl.ds(0, PLANE - 1)], a2_send.at[m])
 
+    def down_block(to, w, slot, zz):
+        rows = pl.ds(pl.multiple_of(zz * PLANE * 2 * CAP, PLANE * 2 * CAP), PLANE * 2 * CAP)
+
+        @pl.loop(0, CW // 256)
+        def _(i):
+            cols = pl.ds(pl.multiple_of(i * 256, 256), 256)
+            part = jnp.dot(hid[rows, :], w[slot, 0, :, cols], preferred_element_type=F32)
+            to[zz, :, :, cols] = part.astype(BF16).reshape(PLANE, 2 * CAP, 256)
+
     def down(to, w, sem, n, slots, count, base):
         slot = lax.rem(n, slots)
         done(w.at[slot, 0], sem.at[slot, 0])
@@ -310,18 +312,93 @@
             part = jnp.dot(hid[...], w[slot, 0, :, cols], preferred_element_type=F32)
             to[:, :, :, cols] = part.astype(BF16).reshape(NZ, PLANE, 2 * CAP, 256)
 
+        refill_down(w, sem, n, slots, count, base)
+
+    def refill_down(w, sem, n, slots, count, base):
         @pl.when(n + slots < count)
         def _():
-            load_down(w, sem, slot, base + n + slots)
+            load_down(w, sem, lax.rem(n, slots), base + n + slots)
 
     def plus(a, b):
         return (a.astype(F32) + b.astype(F32)).astype(BF16)
+
+    def first_send(k):
+        send(y1.at[k, across, low], s1.at[k, 0], s1_send.at[k, 0], s1_recv.at[k, 0], me.z_up)
+        send(y1.at[k, across, high], s1.at[k, 1], s1_send.at[k, 1], s1_recv.at[k, 1], me.z_down)
 
     def first(k):
         left_z(k)
         down(y1.at[k], w1, w1_sem, k, SLOTS1, k1, 0)
-        send(y1.at[k, across, low], s1.at[k, 0], s1_send.at[k, 0], s1_recv.at[k, 0], me.z_up)
-        send(y1.at[k, across, high], s1.at[k, 1], s1_send.at[k, 1], s1_recv.at[k, 1], me.z_down)
+        first_send(k)
+
+    def first_across(k):
+        left_z(k)
+        done(w1.at[k, 0], w1_sem.at[k, 0])
+        down_block(y1.at[k], w1, k, across)
+        first_send(k)
+
+    def first_rest(k):
+        for zz in (me.up, me.down, me.z):
+            down_block(y1.at[k], w1, k, zz)
+        refill_down(w1, w1_sem, k, SLOTS1, k1, 0)
+
+    def other_block(zz):
+        down_block(y2.at[0], w2, 0, zz)
+        here = l2.at[0, zz, me.j]
+        for off in OFFS:
+            j, device = me.plane(off)
+            send(y2.at[0, zz, j], here, b2_send.at[0], b2_recv.at[0], device)
+        pltpu.make_async_copy(y2.at[0, zz, me.j], here, b2_recv.at[0]).start()
+
+    end1, end2 = (k1 - 1) % SLOTS1, (K2 - 1) % SLOTS2
+    block_rows = PLANE * 2 * CAP
+
+    def add_block(zz):
+        rows = pl.ds(pl.multiple_of(zz * block_rows, block_rows), block_rows)
+        for i in range(2):
+            @pl.loop(0, hid.shape[1] // 256)
+            def _(n):
+                cols = pl.ds(pl.multiple_of(n * 256, 256), 256)
+                to = pl.ds(pl.multiple_of(i * hid.shape[1] + n * 256, 256), 256)
+                x = x1[k1 - 1, zz].reshape(block_rows, CW)
+                acc[rows, to] = acc[rows, to] + jnp.dot(x, w1[end1, i, :, cols], preferred_element_type=F32)
+
+    def finish_block(zz):
+        rows = pl.ds(pl.multiple_of(zz * block_rows, block_rows), block_rows)
+
+        @pl.loop(0, hid.shape[1] // 256)
+        def _(n):
+            cols = pl.ds(pl.multiple_of(n * 256, 256), 256)
+            more = pl.ds(pl.multiple_of(hid.shape[1] + n * 256, 256), 256)
+            x = x2[K2 - 1, zz].reshape(block_rows, CW)
+            g = acc[rows, cols] + jnp.dot(x, w2[end2, 0, :, cols], preferred_element_type=F32)
+            u = acc[rows, more] + jnp.dot(x, w2[end2, 1, :, cols], preferred_element_type=F32)
+            hid[rows, cols] = (g / (1.0 + jnp.exp(-g)) * u).astype(BF16)
+
+    for i in range(2):
+        done(w1.at[end1, i], w1_sem.at[end1, i])
+        done(w2.at[end2, i], w2_sem.at[end2, i])
+    for zz in (me.z, me.up, me.down):
+        add_block(zz)
+    done(x1.at[k1 - 1, across, low], f_recv.at[k1 - 1, 0])
+    done(x1.at[k1 - 1, across, high], f_recv.at[k1 - 1, 1])
+    add_block(across)
+    load_down(w1, w1_sem, end1, end1)
+    done(x2.at[K2 - 1], a2_recv.at[K2 - 1])
+    finish_block(across)
+    first_across(0)
+    left_tokens(0)
+    done(w2.at[0, 0], w2_sem.at[0, 0])
+    other_block(across)
+    first_across(1)
+    for zz in (me.up, me.down, me.z):
+        finish_block(zz)
+    load_down(w2, w2_sem, end2, k1 + end2)
+    first_rest(0)
+    for zz in (me.up, me.down, me.z):
+        other_block(zz)
+    refill_down(w2, w2_sem, 0, SLOTS2, K2, k1)
+    first_rest(1)
 
     def second(k):
         done(s1.at[k, 0], s1_recv.at[k, 0])
@@ -396,18 +473,35 @@
         total = u2[m, me.z].astype(F32) + v2[m, 0].astype(F32) + v2[m, 1].astype(F32)
         out[:, pl.ds(pl.multiple_of((k1 + m) * CW, CW), CW)] = total.astype(BF16)
 
-    @pl.loop(0, max(k1 + 7, 4 + 2 * K2))
+    def in_pairs(k, lag, step):
+        for i in range(2):
+            @pl.when((k >= lag) & (2 * (k - lag) + i < k1))
+            def _():
+                step(2 * (k - lag) + i)
+
+    @pl.loop(0, max(k1 + 6, 2 * K2 + 5))
     def _(k):
-        between(k, 0, k1, first)
+        between(k, 2, k1 - 2, lambda i: first(i + 2))
         between(k, 2, k1, second)
-        between(k, 0, K2, other_first)
+        between(k, 0, K2 - 1, lambda i: other_first(i + 1))
         between(k, 3, k1, third)
-        every_second(k, 2, other_second)
-        every_second(k, 3, other_third)
-        every_second(k, 4, other_fourth)
-        every_second(k, 5, other_fifth)
-        between(k, 6, k1, fourth)
-        between(k, 7, k1, fifth)
+        for odd in range(2):
+            @pl.when((k >= 3) & (k % 3 == odd) & (2 * (k // 3 - 1) + odd < K2))
+            def _():
+                other_second(2 * (k // 3 - 1) + odd)
+
+        for at, step in ((k1 + 1, other_third), (k1 + 2, other_fourth)):
+            @pl.when(k == at)
+            def _():
+                pl.loop(0, K2)(step)
+
+        in_pairs(k, k1, fourth)
+
+        @pl.when(k == k1 + 4)
+        def _():
+            pl.loop(0, K2)(other_fifth)
+
+        in_pairs(k, k1 + 1, fifth)
 
     @pl.loop(0, k1)
     def _(k):

time: 213 us -> 204 us (0.958)
  Pallas kernels: 209 us -> 202 us
    pallas_call x1, Pallas kernels: 209 us -> 202 us  [on_device(): pl.pallas_call(functools.partial(kernel, k1), out_shape=jax.ShapeDtypeStr...]
where the time goes in v3:
time: 204 us
  Pallas kernels  202 us (99%)
  local copies, waits for them, and re-layouts  2.16 us (1%)
    pallas_call x1, Pallas kernels, on_device(): pl.pallas_call(functools.partial(kernel, k1), out_shape=jax.ShapeDtypeStr...  202 us

profile of v3, /device:TPU:1, one launch (start us, length us, event | category | flops | bytes accessed | tf_op | source)
XLA Modules:
  0.0 204.2 jit_solution(11915482743616795995)
XLA Ops:
  0.0 202.0 %shard_map.64 = bf16[64,7168]{1,0:T(8,128)(2,1)} custom-call(bf16[64,7168]{1,0:T(8,128)(2,1)} %tok.1, s32[2,64]{1,0:T(2,128)} %bitcast.8, f32[2,64]{1,0:T(2,128)} %bitcast.9, bf16[7168,512]{1,0:T(8,128)(2,1)} %bitcast.5, bf16[7168,512]{1,0:T(8,128)(2,1)} %bitcast.6, bf16[512,7168]{1,0:T(8,128)(2,1)} %bitcast.7), custom_call_target="tpu_custom_call" | custom-call | tf_op jit(solution)/shard_map/pallas_call | solution.py:535
  202.0 2.2 %copy.8 = bf16[64,7168]{1,0:T(8,128)(2,1)} copy(bf16[64,7168]{1,0:T(8,128)(2,1)} %shard_map.64) | data formatting | bytes 1835008

commit v4 on v3

--- a/solution.py
+++ b/solution.py
@@ -49,11 +49,9 @@
         return own
 
 
-def enter(partners):
-    barrier = pltpu.get_barrier_semaphore()
+def greet(partners):
     for device in partners:
-        pl.semaphore_signal(barrier, inc=1, device_id=device, device_id_type=MESH)
-    pl.semaphore_wait(barrier, len(partners))
+        pl.semaphore_signal(pltpu.get_barrier_semaphore(), inc=1, device_id=device, device_id_type=MESH)
 
 
 def send(src, dst, send_sem, recv_sem, device):
@@ -93,6 +91,8 @@
         cols = pl.ds(pl.multiple_of(kk * CW, CW), CW)
         pltpu.make_async_copy(wd_hbm.at[:, cols], w.at[slot, 0], sem.at[slot, 0]).start()
 
+    partners = [me.plane(off)[1] for off in OFFS] + me.column()
+    greet(partners)
     for k in range(SLOTS1):
         load_in(w1, w1_sem, k, k)
     for m in range(SLOTS2):
@@ -110,7 +110,7 @@
     own = jnp.concatenate(parts, axis=0)
     lane_core = lax.broadcasted_iota(jnp.int32, (8, 2 * TOK), 1) // TOK
     meta[...] = jnp.where(lane_core == me.c, jnp.concatenate([own, own], axis=1), 0.0)
-    enter([me.plane(off)[1] for off in OFFS] + me.column())
+    pl.semaphore_wait(pltpu.get_barrier_semaphore(), len(partners))
 
     own_meta = metas.at[me.z, me.c]
     pltpu.make_async_copy(meta, own_meta, m_recv).start()
@@ -213,7 +213,7 @@
             out2[m, zz] = picked.astype(BF16).reshape(PLANE, 2 * CAP, CW)
 
         here = x2.at[m, :, me.j]
-        for off in OFFS:
+        for off in OFFS[::-1]:
             j, device = me.plane(off)
             send(out2.at[m, :, j], here, a2_send.at[m], a2_recv.at[m], device)
         pltpu.make_async_copy(out2.at[m, :, me.j], here, a2_recv.at[m]).start()
@@ -225,7 +225,6 @@
 
     p1_issue(0)
     p1_issue(1)
-    p1_issue(2)
     done(ztok.at[me.down, own_rows], t_recv.at[0])
     part = ztok.at[me.down, pl.ds(pl.multiple_of(me.c * TOK, TOK), half)]
     send(part, part, t_send.at[2], t_recv.at[2], me.z_up)
@@ -233,6 +232,7 @@
     part = ztok.at[me.up, pl.ds(pl.multiple_of(me.c * TOK + half, half), half)]
     send(part, part, t_send.at[3], t_recv.at[3], me.z_down)
     z_issue(0)
+    p1_issue(2)
     p1_issue(3)
     for dz in range(1, NZ):
         pickers(lax.rem(me.z + dz, NZ))
@@ -331,6 +331,14 @@
         down(y1.at[k], w1, w1_sem, k, SLOTS1, k1, 0)
         first_send(k)
 
+    def second(k):
+        done(s1.at[k, 0], s1_recv.at[k, 0])
+        y1[k, me.up, low] = plus(y1[k, me.up, low], s1[k, 0])
+        send(y1.at[k, me.up], s2.at[k, 0], s2_send.at[k, 0], s2_recv.at[k, 0], me.z_up)
+        done(s1.at[k, 1], s1_recv.at[k, 1])
+        y1[k, me.down, high] = plus(y1[k, me.down, high], s1[k, 1])
+        send(y1.at[k, me.down], s2.at[k, 1], s2_send.at[k, 1], s2_recv.at[k, 1], me.z_down)
+
     def first_across(k):
         left_z(k)
         done(w1.at[k, 0], w1_sem.at[k, 0])
@@ -338,9 +346,9 @@
         first_send(k)
 
     def first_rest(k):
-        for zz in (me.up, me.down, me.z):
+        for zz in (me.up, me.down):
             down_block(y1.at[k], w1, k, zz)
-        refill_down(w1, w1_sem, k, SLOTS1, k1, 0)
+        second(k)
 
     def other_block(zz):
         down_block(y2.at[0], w2, 0, zz)
@@ -391,22 +399,18 @@
     done(w2.at[0, 0], w2_sem.at[0, 0])
     other_block(across)
     first_across(1)
-    for zz in (me.up, me.down, me.z):
+    for zz in (me.up, me.down):
         finish_block(zz)
+    first_rest(0)
+    finish_block(me.z)
     load_down(w2, w2_sem, end2, k1 + end2)
-    first_rest(0)
     for zz in (me.up, me.down, me.z):
         other_block(zz)
     refill_down(w2, w2_sem, 0, SLOTS2, K2, k1)
     first_rest(1)
-
-    def second(k):
-        done(s1.at[k, 0], s1_recv.at[k, 0])
-        y1[k, me.up, low] = plus(y1[k, me.up, low], s1[k, 0])
-        send(y1.at[k, me.up], s2.at[k, 0], s2_send.at[k, 0], s2_recv.at[k, 0], me.z_up)
-        done(s1.at[k, 1], s1_recv.at[k, 1])
-        y1[k, me.down, high] = plus(y1[k, me.down, high], s1[k, 1])
-        send(y1.at[k, me.down], s2.at[k, 1], s2_send.at[k, 1], s2_recv.at[k, 1], me.z_down)
+    for k in range(2):
+        down_block(y1.at[k], w1, k, me.z)
+        refill_down(w1, w1_sem, k, SLOTS1, k1, 0)
 
     def third(k):
         done(s2.at[k, 0], s2_recv.at[k, 0])
@@ -479,29 +483,30 @@
             def _():
                 step(2 * (k - lag) + i)
 
-    @pl.loop(0, max(k1 + 6, 2 * K2 + 5))
+    @pl.loop(0, max(k1 + 5, 2 * K2 + 4))
     def _(k):
-        between(k, 2, k1 - 2, lambda i: first(i + 2))
-        between(k, 2, k1, second)
+        between(k, 0, k1 - 2, lambda i: first(i + 2))
+        between(k, 2, k1 - 2, lambda i: second(i + 2))
         between(k, 0, K2 - 1, lambda i: other_first(i + 1))
-        between(k, 3, k1, third)
+        between(k, 1, k1, third)
+        n = k + 1
         for odd in range(2):
-            @pl.when((k >= 3) & (k % 3 == odd) & (2 * (k // 3 - 1) + odd < K2))
+            @pl.when((n >= 3) & (n % 3 == odd) & (2 * (n // 3 - 1) + odd < K2))
             def _():
-                other_second(2 * (k // 3 - 1) + odd)
-
-        for at, step in ((k1 + 1, other_third), (k1 + 2, other_fourth)):
+                other_second(2 * (n // 3 - 1) + odd)
+
+        for at, step in ((k1 - 1, other_third), (k1, other_fourth)):
             @pl.when(k == at)
             def _():
                 pl.loop(0, K2)(step)
 
-        in_pairs(k, k1, fourth)
-
-        @pl.when(k == k1 + 4)
+        in_pairs(k, k1 - 1, fourth)
+
+        @pl.when(k == k1 + 3)
         def _():
             pl.loop(0, K2)(other_fifth)
 
-        in_pairs(k, k1 + 1, fifth)
+        in_pairs(k, k1, fifth)
 
     @pl.loop(0, k1)
     def _(k):

time: 204 us -> 200 us (0.980)
  Pallas kernels: 202 us -> 198 us
    pallas_call x1, Pallas kernels: 202 us -> 198 us  [on_device(): pl.pallas_call(functools.partial(kernel, k1), out_shape=jax.ShapeDtypeStr...]
where the time goes in v4:
time: 200 us
  Pallas kernels  198 us (99%)
  local copies, waits for them, and re-layouts  2.16 us (1%)
    pallas_call x1, Pallas kernels, on_device(): pl.pallas_call(functools.partial(kernel, k1), out_shape=jax.ShapeDtypeStr...  198 us

profile of v4, /device:TPU:1, one launch (start us, length us, event | category | flops | bytes accessed | tf_op | source)
XLA Modules:
  0.0 200.3 jit_solution(6795801286979499980)
XLA Ops:
  0.0 198.2 %shard_map.64 = bf16[64,7168]{1,0:T(8,128)(2,1)} custom-call(bf16[64,7168]{1,0:T(8,128)(2,1)} %tok.1, s32[2,64]{1,0:T(2,128)} %bitcast.8, f32[2,64]{1,0:T(2,128)} %bitcast.9, bf16[7168,512]{1,0:T(8,128)(2,1)} %bitcast.5, bf16[7168,512]{1,0:T(8,128)(2,1)} %bitcast.6, bf16[512,7168]{1,0:T(8,128)(2,1)} %bitcast.7), custom_call_target="tpu_custom_call" | custom-call | tf_op jit(solution)/shard_map/pallas_call | solution.py:540
  198.2 2.2 %copy.8 = bf16[64,7168]{1,0:T(8,128)(2,1)} copy(bf16[64,7168]{1,0:T(8,128)(2,1)} %shard_map.64) | data formatting | bytes 1835008

commit v5 on v4

--- a/solution.py
+++ b/solution.py
@@ -371,7 +371,7 @@
                 x = x1[k1 - 1, zz].reshape(block_rows, CW)
                 acc[rows, to] = acc[rows, to] + jnp.dot(x, w1[end1, i, :, cols], preferred_element_type=F32)
 
-    def finish_block(zz):
+    def finish_block(zz, both=False):
         rows = pl.ds(pl.multiple_of(zz * block_rows, block_rows), block_rows)
 
         @pl.loop(0, hid.shape[1] // 256)
@@ -381,6 +381,10 @@
             x = x2[K2 - 1, zz].reshape(block_rows, CW)
             g = acc[rows, cols] + jnp.dot(x, w2[end2, 0, :, cols], preferred_element_type=F32)
             u = acc[rows, more] + jnp.dot(x, w2[end2, 1, :, cols], preferred_element_type=F32)
+            if both:
+                x = x1[k1 - 1, zz].reshape(block_rows, CW)
+                g = g + jnp.dot(x, w1[end1, 0, :, cols], preferred_element_type=F32)
+                u = u + jnp.dot(x, w1[end1, 1, :, cols], preferred_element_type=F32)
             hid[rows, cols] = (g / (1.0 + jnp.exp(-g)) * u).astype(BF16)
 
     for i in range(2):
@@ -390,10 +394,9 @@
         add_block(zz)
     done(x1.at[k1 - 1, across, low], f_recv.at[k1 - 1, 0])
     done(x1.at[k1 - 1, across, high], f_recv.at[k1 - 1, 1])
-    add_block(across)
+    done(x2.at[K2 - 1], a2_recv.at[K2 - 1])
+    finish_block(across, True)
     load_down(w1, w1_sem, end1, end1)
-    done(x2.at[K2 - 1], a2_recv.at[K2 - 1])
-    finish_block(across)
     first_across(0)
     left_tokens(0)
     done(w2.at[0, 0], w2_sem.at[0, 0])
@@ -483,7 +486,7 @@
             def _():
                 step(2 * (k - lag) + i)
 
-    @pl.loop(0, max(k1 + 5, 2 * K2 + 4))
+    @pl.loop(0, max(k1 + 6, 2 * K2 + 5))
     def _(k):
         between(k, 0, k1 - 2, lambda i: first(i + 2))
         between(k, 2, k1 - 2, lambda i: second(i + 2))
@@ -500,13 +503,13 @@
             def _():
                 pl.loop(0, K2)(step)
 
-        in_pairs(k, k1 - 1, fourth)
-
-        @pl.when(k == k1 + 3)
+        in_pairs(k, k1, fourth)
+
+        @pl.when(k == k1 + 4)
         def _():
             pl.loop(0, K2)(other_fifth)
 
-        in_pairs(k, k1, fifth)
+        in_pairs(k, k1 + 1, fifth)
 
     @pl.loop(0, k1)
     def _(k):

time: 200 us -> 200 us (level)
  no operation moved by 1% of the time
where the time goes in v5:
time: 200 us
  Pallas kernels  197 us (98%)
  local copies, waits for them, and re-layouts  2.16 us (1%)
    pallas_call x1, Pallas kernels, on_device(): pl.pallas_call(functools.partial(kernel, k1), out_shape=jax.ShapeDtypeStr...  197 us

profile of v5, /device:TPU:1, one launch (start us, length us, event | category | flops | bytes accessed | tf_op | source)
XLA Modules:
  0.0 199.5 jit_solution(9557998423766554141)
XLA Ops:
  0.0 197.4 %shard_map.64 = bf16[64,7168]{1,0:T(8,128)(2,1)} custom-call(bf16[64,7168]{1,0:T(8,128)(2,1)} %tok.1, s32[2,64]{1,0:T(2,128)} %bitcast.8, f32[2,64]{1,0:T(2,128)} %bitcast.9, bf16[7168,512]{1,0:T(8,128)(2,1)} %bitcast.5, bf16[7168,512]{1,0:T(8,128)(2,1)} %bitcast.6, bf16[512,7168]{1,0:T(8,128)(2,1)} %bitcast.7), custom_call_target="tpu_custom_call" | custom-call | tf_op jit(solution)/shard_map/pallas_call | solution.py:543
  197.4 2.2 %copy.8 = bf16[64,7168]{1,0:T(8,128)(2,1)} copy(bf16[64,7168]{1,0:T(8,128)(2,1)} %shard_map.64) | data formatting | bytes 1835008

commit v6 on v5

--- a/solution.py
+++ b/solution.py
@@ -528,6 +528,16 @@
             done(v2.at[m, 0], v2_send.at[m, side])
 
 
+def hand_over(result, out, sem):
+    copies = [
+        pltpu.make_async_copy(result.at[pl.ds(i * 16, 16)], out.at[pl.ds(i * 16, 16)], sem.at[i]) for i in range(TOK // 16)
+    ]
+    for copy in copies:
+        copy.start()
+    for copy in copies:
+        copy.wait()
+
+
 def on_device(tokens, routes, gates, w_gate, w_up, w_down):
     width = tokens.shape[1]
     k1 = width // CW - K2
@@ -540,7 +550,7 @@
 
     vmem = pl.BlockSpec(memory_space=pltpu.VMEM)
     hbm = pl.BlockSpec(memory_space=pl.ANY)
-    return pl.pallas_call(
+    result = pl.pallas_call(
         functools.partial(kernel, k1),
         out_shape=jax.ShapeDtypeStruct(tokens.shape, BF16),
         in_specs=[vmem, vmem, vmem, hbm, hbm, hbm],
@@ -577,6 +587,13 @@
         ],
         compiler_params=pltpu.CompilerParams(collective_id=0, has_side_effects=True, vmem_limit_bytes=61 << 20),
     )(tokens, routes.T, gates.T, w_gate[0], w_up[0], w_down[0])
+    return pl.pallas_call(
+        hand_over,
+        out_shape=jax.ShapeDtypeStruct(tokens.shape, BF16),
+        in_specs=[hbm],
+        out_specs=hbm,
+        scratch_shapes=[dma(4)],
+    )(result)
 
 
 def solution(mesh):

time: 200 us -> 226 us (1.13)
  Pallas kernels: 197 us -> 226 us
    pallas_call x0 -> x1, Pallas kernels: none -> 28.9 us  [on_device(): pl.pallas_call(hand_over, out_shape=jax.ShapeDtypeStruct(tokens.shape, BF...]
where the time goes in v6:
time: 226 us
  Pallas kernels  226 us (100%)
    pallas_call x1, Pallas kernels, on_device(): pl.pallas_call(functools.partial(kernel, k1), out_shape=jax.ShapeDtypeStr...  197 us
    pallas_call x1, Pallas kernels, on_device(): pl.pallas_call(hand_over, out_shape=jax.ShapeDtypeStruct(tokens.shape, BF...  28.9 us

profile of v6, /device:TPU:1, one launch (start us, length us, event | category | flops | bytes accessed | tf_op | source)
XLA Modules:
  0.0 226.3 jit_solution(7370020157342378141)
XLA Ops:
  0.0 197.4 %shard_map.64.result = bf16[64,7168]{1,0:T(8,128)(2,1)} custom-call(bf16[64,7168]{1,0:T(8,128)(2,1)} %tok.1, s32[2,64]{1,0:T(2,128)} %bitcast.8, f32[2,64]{1,0:T(2,128)} %bitcast.9, bf16[7168,512]{1,0:T(8,128)(2,1)} %bitcast.5, bf16[7168,512]{1,0:T(8,128)(2,1)} %bitcast.6, bf16[512,7168]{1,0:T(8,128)(2,1)} %bitcast.7), custom_call_target="tpu_custom_call" | custom-call | tf_op jit(solution)/shard_map/pallas_call | solution.py:553
  197.4 28.9 %shard_map.65 = bf16[64,7168]{1,0:T(8,128)(2,1)} custom-call(bf16[64,7168]{1,0:T(8,128)(2,1)} %shard_map.64.result), custom_call_target="tpu_custom_call" | custom-call | tf_op jit(solution)/shard_map/pallas_call | solution.py:590
